TPU v7x, 32 devices: a whole 2x2x4 slice. The times are simulated.
32 devices in a mesh: grp: 2 (over y), seq: 4 (over z), tp: 2 (over x), sub: 2 (over core).
Axes of the slice: x: 2, y: 2, z: 4, core: 2. Of those that a mesh axis runs over, the one named last changes fastest.
Arguments:
- acts: bfloat16 [16384, 4096], P(('grp', 'seq', 'sub'), 'tp'), parts along dimension 0, may hold values from -6 to 6
- out_grads: bfloat16 [16384, 14336], P(('grp', 'seq', 'sub'), 'tp'), parts along dimension 0, may hold values from -6 to 6
- proj_in: bfloat16 [4096, 64], P('tp'), may hold values from -0.09375 to 0.09375
- proj_out: bfloat16 [14336, 64], P('tp'), may hold values from -0.046875 to 0.046875
- seq_lengths: int32 [16, 16], P(('grp', 'seq', 'sub')), parts along dimension 0, may hold values from 1 to 256, 1024 in all within a row
- hard_ids: int32 [16, 8], P(('grp', 'seq', 'sub')), parts along dimension 0, may hold values from 0 to 15
- slots: int32 [128], P(('grp', 'seq', 'sub')), parts along dimension 0, may hold values from 0 to 63, each once
Outputs:
- features: float32 [128, 4096], P(('grp', 'seq', 'sub'), 'tp'), parts along dimension 0
There are 2 independent parts, one for each index of `grp`. A program takes and returns all parts, laid end to end along the dimension named above; an argument that names none is the same for every part. Nothing has to cross between parts.
Inputs may be any that keep to these rules, and one draw needn't show every extreme that they name: `slots`: each example's row, every row once. `hard_ids`: repeats allowed.
All inputs are finite; a program needn't handle non-finite values.
Results may differ from a plain program's by a relative error of at most 0.0003.
Values sent between devices are 32-bit elements; how exact they have to be, the bound alone decides.
A program may use at most 64 MiB of HBM per device.

v0:
```python
import jax
import jax.numpy as jnp
from jax import lax
from jax.sharding import PartitionSpec as P


def example_masks(first, after, count):
    position = jnp.arange(count, dtype=jnp.int32)
    return ((position[None, :] >= first[:, None]) & (position[None, :] < after[:, None])).astype(
        jnp.float32
    )


def masked_outer(masks, left_rows, right_rows):
    weighted = masks[:, :, None] * left_rows[None, :, :]
    return jnp.einsum(
        "kti,tj->kij",
        weighted,
        right_rows,
        precision=lax.Precision.HIGHEST,
        preferred_element_type=jnp.float32,
    )


def body(acts, out_grads, proj_in, proj_out, seq_lengths, hard_ids, slots):
    tp_count = lax.axis_size("tp")
    share = proj_in.shape[1] // tp_count
    rank_full = proj_in.shape[1]
    part_acts = jnp.dot(acts, proj_in, preferred_element_type=jnp.float32)
    part_grads = jnp.dot(out_grads, proj_out, preferred_element_type=jnp.float32)
    lengths = seq_lengths[0]
    ends = jnp.cumsum(lengths)
    starts = ends - lengths
    select = (
        hard_ids[0][:, None] == jnp.arange(lengths.shape[0], dtype=jnp.int32)[None, :]
    ).astype(jnp.int32)
    first = jnp.sum(select * starts[None, :], axis=1)
    after = jnp.sum(select * ends[None, :], axis=1)
    hard_count = hard_ids.shape[1]
    token_count = acts.shape[0]
    summed_acts, summed_grads = lax.psum((part_acts, part_grads), "tp")
    mine_acts = lax.dynamic_slice_in_dim(summed_acts, lax.axis_index("tp") * share, share, 1)
    masks = example_masks(first, after, token_count)
    gradient = masked_outer(masks, mine_acts, summed_grads)
    local_feats = gradient.reshape(hard_count, share * rank_full)
    slot_values = slots.astype(jnp.float32)
    owned_rows = (
        lax.axis_index(("seq", "sub")) * hard_count + jnp.arange(hard_count, dtype=jnp.int32)
    ).astype(jnp.float32)
    feat_piece = lax.all_gather(local_feats, ("seq", "sub"), axis=0, tiled=True)
    slot_piece = lax.all_gather(slot_values, ("seq", "sub"), axis=0, tiled=True)
    picker = (owned_rows[:, None] == slot_piece[None, :]).astype(jnp.float32)
    return jnp.dot(picker, feat_piece, precision=lax.Precision.HIGHEST)


def solution(mesh):
    placed = (
        P(("grp", "seq", "sub"), "tp"),
        P(("grp", "seq", "sub"), "tp"),
        P("tp", None),
        P("tp", None),
        P(("grp", "seq", "sub"), None),
        P(("grp", "seq", "sub"), None),
        P(("grp", "seq", "sub")),
    )
    return jax.shard_map(
        body, mesh=mesh, in_specs=placed, out_specs=P(("grp", "seq", "sub"), "tp"), check_vma=False
    )
```

profile of v0, /device:TPU:0, one launch (start us, length us, event | category | flops | bytes accessed | tf_op | source)
XLA Modules:
  0.0 78.6 jit_solution(8896014044093512958)
XLA Ops:
  6.5 0.0 copy-start
  6.5 0.0 copy-start.4
  6.5 0.0 all-reduce.4.cloned.1.call-start
  6.6 4.4 %fusion.12 = f32[1024,64]{0,1:T(8,128)} fusion(bf16[1024,2048]{1,0:T(8,128)(2,1)} %param.7, bf16[2048,64]{0,1:T(8,128)(2,1)} %param.9), kind=kOutput, calls=%fused_computation.21 | convolution fusion | flops 268435456 | bytes 4718592 | tf_op jit(solution)/shard_map/dot_general | solution.py:29
  11.0 0.0 copy-done
  11.0 10.4 %fusion.13 = f32[1024,64]{0,1:T(8,128)} fusion(bf16[1024,7168]{1,0:T(8,128)(2,1)} %param.8, bf16[7168,64]{0,1:T(8,128)(2,1)S(1)} %copy-done), kind=kOutput, calls=%fused_computation.22 | convolution fusion | flops 939524096 | bytes 15859712 | tf_op jit(solution)/shard_map/dot_general | solution.py:30
  21.4 0.0 all-reduce.4.cloned.1.call-update
  21.5 0.0 copy-done.1
  21.5 0.1 copy.10
  21.6 0.1 reduce
  21.7 0.0 copy-done.4
  21.7 0.6 dynamic-slice
  23.0 0.0 copy-done.3
  23.0 0.1 convert_dynamic-update-slice_fusion
  23.1 18.1 %all-reduce = f32[64]{0:T(128)S(1)} all-reduce(f32[64]{0:T(128)S(1)} %convert_dynamic-update-slice_fusion), channel_id=1, replica_groups=mesh['grp'=2,'seq'=4,'tp'=2,'sub'=2] {'seq','sub'}, use_global_device_ids=true, to_apply=%add | all-reduce | flops 64 | bytes 512
  41.1 0.0 copy-done.2
  41.1 0.2 select_reduce_fusion.1
  41.3 0.1 fusion.6
  41.4 11.7 %all-reduce.4.cloned.1.call-done = (f32[1024,64]{0,1:T(8,128)}, f32[1024,64]{0,1:T(8,128)}) async-done(((f32[1024,64]{0,1:T(8,128)}, f32[1024,64]{0,1:T(8,128)}), (f32[1024,64]{0,1:T(8,128)}, f32[1024,64]{0,1:T(8,128)})) %all-reduce.4.cloned.1.call-update) | async-done | bytes 524304 | tf_op jit(solution)/shard_map/psum | solution.py:41
  53.1 0.9 %constant_dynamic-slice_fusion = f32[1024,32]{0,1:T(8,128)S(1)} fusion(f32[1024,64]{0,1:T(8,128)} %get-tuple-element.7, s32[]{:T(128)S(6)} %select_n.3), kind=kLoop, calls=%fused_computation.20 | loop fusion | bytes 262148 | tf_op jit(solution)/shard_map/dynamic_slice | solution.py:42
  54.0 1.9 %fusion = f32[8,32,64]{2,1,0:T(8,128)S(1)} fusion(f32[1024,32]{0,1:T(8,128)S(1)} %constant_dynamic-slice_fusion, f32[8,1024]{1,0:T(8,128)S(1)} %fusion.6, f32[1024,64]{0,1:T(8,128)} %get-tuple-element.8), kind=kOutput, calls=%fused_computation | convolution fusion | flops 201588736 | bytes 491520 | tf_op jit(solution)/shard_map/kti,tj->kij/dot_general | solution.py:16
  56.0 0.1 reshape.67
  56.1 14.8 %all_gather.7 = f32[64,2048]{1,0:T(8,128)S(1)} all-gather(f32[8,2048]{1,0:T(8,128)S(1)} %reshape.67), channel_id=1, replica_groups=mesh['grp'=2,'seq'=4,'tp'=2,'sub'=2] {'seq','sub'}, dimensions={0}, use_global_device_ids=true | all-gather | bytes 589824 | tf_op jit(solution)/shard_map/all_gather | solution.py:50
  70.8 0.9 %fusion.7 = f32[8,2048]{1,0:T(8,128)} fusion(f32[64,2048]{1,0:T(8,128)S(1)} %all_gather.7, f32[64]{0:T(128)S(1)} %all-reduce, f32[8]{0:T(128)S(1)} %add_convert_fusion), kind=kOutput, calls=%fused_computation.12 | convolution fusion | flops 12583424 | bytes 590112 | tf_op jit(solution)/shard_map/dot_general | solution.py:53
  (7 shorter events, 0.1 us)
Async XLA Ops:
  6.5 4.4 %copy-start = (bf16[7168,64]{0,1:T(8,128)(2,1)S(1)}, bf16[7168,64]{0,1:T(8,128)(2,1)}, u32[]{:S(2)}) copy-start(bf16[7168,64]{0,1:T(8,128)(2,1)} %param.10) | copy-start | bytes 2752516
  6.5 15.2 %copy-start.4 = (u32[32]{0:T(128)S(1)}, u32[32]{0:T(128)}, u32[]{:S(2)}) copy-start(u32[32]{0:T(128)} %constant.31) | copy-start | bytes 388
  6.5 14.9 %copy-start.1 = (s32[1,16]{1,0:T(1,128)S(1)}, s32[1,16]{1,0:T(1,128)}, u32[]{:S(2)}) copy-start(s32[1,16]{1,0:T(1,128)} %param.11) | copy-start | bytes 196
  6.5 16.4 %copy-start.3 = (s32[8]{0:T(128)S(1)}, s32[8]{0:T(128)}, u32[]{:S(2)}) copy-start(s32[8]{0:T(128)} %param.13) | copy-start | bytes 100
  6.5 34.6 %copy-start.2 = (s32[1,8]{1,0:T(1,128)S(1)}, s32[1,8]{1,0:T(1,128)}, u32[]{:S(2)}) copy-start(s32[1,8]{1,0:T(1,128)} %param.12) | copy-start | bytes 100
  6.5 46.6 %all-reduce.4.cloned.1.call-start = ((), (), s32[]{:S(2)}) async-start(), calls=%async_computation | async-start | bytes 1048576 | tf_op jit(solution)/shard_map/psum | solution.py:41
Sparse Core Ops, SparseCore 0:
  21.6 31.5 all-reduce.3
where the time goes:
time: 78.8 us; the launch traced here: 78.6 us
  blocking collectives  32.8 us (42%)
  matrix products  17.7 us (22%)
  between operations  14.1 us (18%)
  waiting for transfers between devices  11.7 us (15%)
  local copies, waits for them, and re-layouts  1.7 us (2%)
    unnamed x1, blocking collectives  18.1 us
    all_gather x1, blocking collectives, body(): feat_piece = lax.all_gather(local_feats, ('seq', 'sub'), axis=0, tiled=True)  14.8 us
    psum x1, waiting for transfers between devices, body(): summed_acts, summed_grads = lax.psum((part_acts, part_grads), 'tp')  11.7 us
    dot_general x1, matrix products, body(): jnp.dot(out_grads, proj_out, preferred_element_type=jnp.float32)  10.4 us
    dot_general x1, matrix products, body(): part_acts = jnp.dot(acts, proj_in, preferred_element_type=jnp.float32)  4.38 us
    dot_general x1, matrix products, masked_outer(): jnp.einsum('kti,tj->kij', weighted, right_rows, precision=lax.Precision.H...  1.92 us
  transfers between devices with their start and end apart: 1, of which 1 were waited for; matrix products, arithmetic and copies ran while one was open for 2% of the time, Pallas kernels for 0%

commit v1 on v0

v1 whole, which is shorter than its diff:
```python
import jax
import jax.numpy as jnp
from jax import lax
from jax.experimental import pallas as pl
from jax.experimental.pallas import tpu as pltpu
from jax.sharding import PartitionSpec as P

MESH = pl.DeviceIdType.MESH
CHUNK = 256


def project(rows, turned):
    return lax.dot_general(
        rows, turned, (((1,), (1,)), ((), ())), preferred_element_type=jnp.float32
    )


def kernel(
    n_seq, n_sub, n_tp,
    acts, grads, w_in, w_out, lengths, ids, slots,
    out,
    acts_v, grads_v, w_in_v, w_out_v,
    a_own, a_got, g_own, g_got, acc, gath, slot_all,
    load_sem, a_send, a_recv, g_send, g_recv, s_send, s_recv, f_send, f_recv, h_send,
):
    seq, sub, tp = lax.axis_index("seq"), lax.axis_index("sub"), lax.axis_index("tp")
    ranks = n_seq * n_sub
    rank = seq * n_sub + sub
    chunks = acts.shape[0] // CHUNK
    share = a_own.shape[2]
    hard = ids.shape[1]
    count = lengths.shape[1]
    half = CHUNK // 2
    rank_full = w_in.shape[0]

    load_w_in = pltpu.make_async_copy(w_in, w_in_v, load_sem.at[0])
    load_w_out = pltpu.make_async_copy(w_out, w_out_v, load_sem.at[1])
    load_acts, load_grads = [], []
    for c in range(chunks):
        rows = pl.ds(c * CHUNK, CHUNK)
        load_acts.append(pltpu.make_async_copy(acts.at[rows], acts_v.at[rows], load_sem.at[2 + c]))
        load_grads.append(
            pltpu.make_async_copy(grads.at[rows], grads_v.at[rows], load_sem.at[2 + chunks + c])
        )
    load_w_in.start()
    for copy in load_acts:
        copy.start()
    load_w_out.start()
    for copy in load_grads:
        copy.start()

    barrier = pltpu.get_barrier_semaphore()
    for d in range(1, n_tp):
        pl.semaphore_signal(
            barrier, inc=1, device_id={"tp": lax.rem(tp + d, n_tp)}, device_id_type=MESH
        )
    for d in range(1, ranks):
        peer = lax.rem(rank + d, ranks)
        pl.semaphore_signal(
            barrier,
            inc=1,
            device_id={"seq": peer // n_sub, "sub": lax.rem(peer, n_sub)},
            device_id_type=MESH,
        )
    firsts = [jnp.int32(0)] * hard
    afters = [jnp.int32(0)] * hard
    chosen = [ids[0, k] for k in range(hard)]
    start = jnp.int32(0)
    for s in range(count):
        end = start + lengths[0, s]
        for k in range(hard):
            firsts[k] = jnp.where(chosen[k] == s, start, firsts[k])
            afters[k] = jnp.where(chosen[k] == s, end, afters[k])
        start = end
    tile_lane = lax.broadcasted_iota(jnp.int32, slot_all.shape[1:], 1)
    tile = jnp.full(slot_all.shape[1:], -1, jnp.int32)
    for k in range(hard):
        tile = jnp.where(tile_lane == rank * hard + k, slots[k], tile)
    slot_all[rank] = tile
    pl.semaphore_wait(barrier, n_tp - 1 + ranks - 1)

    slot_copies = []
    for d in range(1, ranks):
        peer = lax.rem(rank + d, ranks)
        copy = pltpu.make_async_remote_copy(
            src_ref=slot_all.at[rank],
            dst_ref=slot_all.at[rank],
            send_sem=s_send.at[d - 1],
            recv_sem=s_recv.at[d - 1],
            device_id={"seq": peer // n_sub, "sub": lax.rem(peer, n_sub)},
            device_id_type=MESH,
        )
        copy.start()
        slot_copies.append(copy)

    a_copies, g_copies = [], []
    load_w_in.wait()
    for c in range(chunks):
        load_acts[c].wait()
        part = project(acts_v[c * CHUNK:(c + 1) * CHUNK, :], w_in_v[...])
        turned = part.T
        for q in range(n_tp):
            a_own[c, q] = turned[q * share:(q + 1) * share, :]
        for d in range(1, n_tp):
            to = lax.rem(tp + d, n_tp)
            copy = pltpu.make_async_remote_copy(
                src_ref=a_own.at[c, to],
                dst_ref=a_got.at[d - 1, c],
                send_sem=a_send.at[d - 1, c],
                recv_sem=a_recv.at[d - 1, c],
                device_id={"tp": to},
                device_id_type=MESH,
            )
            copy.start()
            a_copies.append(copy)
    load_w_out.wait()
    for c in range(chunks):
        load_grads[c].wait()
        part = project(grads_v[c * CHUNK:(c + 1) * CHUNK, :], w_out_v[...])
        g_own[c] = jnp.concatenate([part[:half], part[half:]], axis=1)
        for d in range(1, n_tp):
            copy = pltpu.make_async_remote_copy(
                src_ref=g_own.at[c],
                dst_ref=g_got.at[d - 1, c],
                send_sem=g_send.at[d - 1, c],
                recv_sem=g_recv.at[d - 1, c],
                device_id={"tp": lax.rem(tp + d, n_tp)},
                device_id_type=MESH,
            )
            copy.start()
            g_copies.append(copy)

    for copy in slot_copies:
        copy.wait()
    every = slot_all[0]
    for other in range(1, ranks):
        every = jnp.maximum(every, slot_all[other])
    wanted = rank * hard + lax.broadcasted_iota(jnp.int32, every.shape, 0)
    picker = jnp.where(every == wanted, 1.0, 0.0)[:, :ranks * hard].astype(jnp.bfloat16)

    position = lax.broadcasted_iota(jnp.int32, (share, CHUNK), 1)
    lane = lax.broadcasted_iota(jnp.int32, (half, 2 * rank_full), 1)
    for c in range(chunks):
        for d in range(n_tp - 1):
            a_copies[c * (n_tp - 1) + d].wait()
        left = a_own[c, tp]
        for d in range(n_tp - 1):
            left = left + a_got[d, c]
        pieces = []
        for k in range(hard):
            inside = (position >= firsts[k] - c * CHUNK) & (position < afters[k] - c * CHUNK)
            pieces.append(jnp.where(inside, left, 0.0))
        left = jnp.concatenate(pieces, axis=0)
        left_hi = left.astype(jnp.bfloat16)
        left_lo = (left - left_hi.astype(jnp.float32)).astype(jnp.bfloat16)
        for d in range(n_tp - 1):
            g_copies[c * (n_tp - 1) + d].wait()
        pair = g_own[c]
        for d in range(n_tp - 1):
            pair = pair + g_got[d, c]
        swapped = pltpu.roll(pair, rank_full, 1)
        right = jnp.concatenate(
            [jnp.where(lane < rank_full, pair, swapped), jnp.where(lane < rank_full, swapped, pair)],
            axis=0,
        )
        right_hi = right.astype(jnp.bfloat16)
        right_lo = (right - right_hi.astype(jnp.float32)).astype(jnp.bfloat16)
        both = jnp.dot(
            left_hi,
            jnp.concatenate([right_hi, right_lo], axis=1),
            preferred_element_type=jnp.float32,
        )
        total = (
            both[:, :2 * rank_full]
            + both[:, 2 * rank_full:]
            + jnp.dot(left_lo, right_hi, preferred_element_type=jnp.float32)
        )
        if c == 0:
            acc[...] = total
        else:
            acc[...] += total
    out_lane = lax.broadcasted_iota(jnp.int32, (hard, 2 * rank_full), 1)
    mine = pl.ds(pl.multiple_of(rank * hard, hard), hard)
    for j in range(share // 2):
        even = acc[pl.ds(2 * j, hard, stride=share), :]
        odd = acc[pl.ds(2 * j + 1, hard, stride=share), :]
        gath[mine, j * 128:(j + 1) * 128] = jnp.where(out_lane < rank_full, even, odd)

    to_chips, to_cores = [], []
    for d in range(1, n_seq):
        copy = pltpu.make_async_remote_copy(
            src_ref=gath.at[mine],
            dst_ref=gath.at[mine],
            send_sem=f_send.at[d - 1],
            recv_sem=f_recv.at[d - 1],
            device_id={"seq": lax.rem(seq + d, n_seq)},
            device_id_type=MESH,
        )
        copy.start()
        to_chips.append(copy)
    for d in range(n_seq):
        if d:
            to_chips[d - 1].wait_recv()
        owner = lax.rem(seq + n_seq - d, n_seq) * n_sub + sub
        block = pl.ds(pl.multiple_of(owner * hard, hard), hard)
        for b in range(1, n_sub):
            copy = pltpu.make_async_remote_copy(
                src_ref=gath.at[block],
                dst_ref=gath.at[block],
                send_sem=h_send.at[b - 1, 0, d],
                recv_sem=h_send.at[b - 1, 1, d],
                device_id={"sub": lax.rem(sub + b, n_sub)},
                device_id_type=MESH,
            )
            copy.start()
            to_cores.append(copy)
    for copy in to_chips:
        copy.wait_send()
    for copy in to_cores:
        copy.wait()
    every = gath[...]
    high = every.astype(jnp.bfloat16)
    low = (every - high.astype(jnp.float32)).astype(jnp.bfloat16)
    out[...] = jnp.dot(picker, high, preferred_element_type=jnp.float32) + jnp.dot(
        picker, low, preferred_element_type=jnp.float32
    )


def body(acts, grads, w_in, w_out, lengths, ids, slots):
    n_seq, n_sub, n_tp = (lax.axis_size(name) for name in ("seq", "sub", "tp"))
    tokens, features = acts.shape
    hidden = grads.shape[1]
    rank_full = w_in.shape[1]
    w_in, w_out = w_in.T, w_out.T
    share = rank_full // n_tp
    hard = ids.shape[1]
    chunks = tokens // CHUNK
    ranks = n_seq * n_sub
    f32 = jnp.float32
    dma = pltpu.SemaphoreType.DMA
    hbm = pl.BlockSpec(memory_space=pl.ANY)
    smem = pl.BlockSpec(memory_space=pltpu.SMEM)

    def run(*refs):
        kernel(n_seq, n_sub, n_tp, *refs)

    return pl.pallas_call(
        run,
        out_shape=jax.ShapeDtypeStruct((hard, share * rank_full), f32),
        in_specs=[hbm] * 4 + [smem] * 3,
        out_specs=pl.BlockSpec(memory_space=pltpu.VMEM),
        scratch_shapes=[
            pltpu.VMEM((tokens, features), acts.dtype),
            pltpu.VMEM((tokens, hidden), grads.dtype),
            pltpu.VMEM(w_in.shape, w_in.dtype),
            pltpu.VMEM(w_out.shape, w_out.dtype),
            pltpu.VMEM((chunks, n_tp, share, CHUNK), f32),
            pltpu.VMEM((n_tp - 1, chunks, share, CHUNK), f32),
            pltpu.VMEM((chunks, CHUNK // 2, 2 * rank_full), f32),
            pltpu.VMEM((n_tp - 1, chunks, CHUNK // 2, 2 * rank_full), f32),
            pltpu.VMEM((hard * share, 2 * rank_full), f32),
            pltpu.VMEM((ranks * hard, share * rank_full), f32),
            pltpu.VMEM((ranks, hard, -(-ranks * hard // 128) * 128), jnp.int32),
            dma((2 + 2 * chunks,)),
            dma((n_tp - 1, chunks)),
            dma((n_tp - 1, chunks)),
            dma((n_tp - 1, chunks)),
            dma((n_tp - 1, chunks)),
            dma((ranks - 1,)),
            dma((ranks - 1,)),
            dma((n_seq - 1,)),
            dma((n_seq - 1,)),
            dma((n_sub - 1, 2, n_seq)),
        ],
        compiler_params=pltpu.CompilerParams(
            collective_id=0, has_side_effects=True, vmem_limit_bytes=48 * 2**20
        ),
        cost_estimate=pl.CostEstimate(
            flops=2 * tokens * (features + hidden) * rank_full,
            bytes_accessed=2 * tokens * (features + hidden),
            transcendentals=0,
        ),
    )(acts, grads, w_in, w_out, lengths, ids, slots)


def solution(mesh):
    placed = (
        P(("grp", "seq", "sub"), "tp"),
        P(("grp", "seq", "sub"), "tp"),
        P("tp", None),
        P("tp", None),
        P(("grp", "seq", "sub"), None),
        P(("grp", "seq", "sub"), None),
        P(("grp", "seq", "sub")),
    )
    return jax.shard_map(
        body, mesh=mesh, in_specs=placed, out_specs=P(("grp", "seq", "sub"), "tp"), check_vma=False
    )
```

time: 78.8 us -> 35.7 us (0.45)
  blocking collectives: 32.8 us -> 0 us
  Pallas kernels: 0 us -> 28.5 us
  matrix products: 17.7 us -> 0 us
  between operations: 14.1 us -> 0.02 us
  waiting for transfers between devices: 11.7 us -> 0 us
  local copies, waits for them, and re-layouts: 1.7 us -> 6.91 us
    pallas_call x0 -> x1, Pallas kernels: none -> 28.5 us  [body(): pl.pallas_call(run, out_shape=jax.ShapeDtypeStruct((hard, share * rank_fu...]
    unnamed x1 -> x0, blocking collectives: 18.1 us -> none
    dot_general x4 -> x0, matrix products: 17.7 us -> none  [the longest x1 10.4 us: body(): jnp.dot(out_grads, proj_out, preferred_element_type=jnp.float32)]
    all_gather x1 -> x0, blocking collectives: 14.8 us -> none  [body(): feat_piece = lax.all_gather(local_feats, ('seq', 'sub'), axis=0, tiled=True)]
    psum x1 -> x0, waiting for transfers between devices: 11.7 us -> none  [body(): summed_acts, summed_grads = lax.psum((part_acts, part_grads), 'tp')]
    unnamed x12 -> x13, local copies, waits for them, and re-layouts: 0.61 us -> 6.91 us
    dynamic_slice x1 -> x0, local copies, waits for them, and re-layouts: 0.91 us -> none  [body(): lax.dynamic_slice_in_dim(summed_acts, lax.axis_index('tp') * share, share...]
  transfers between devices with their start and end apart: 1 -> 0, of which waited for: 1 -> 0; matrix products, arithmetic and copies ran while one was open for 2% -> 0% of each run, Pallas kernels for 0% -> 0%
where the time goes in v1:
time: 35.7 us; the launch traced here: 35.5 us
  Pallas kernels  28.5 us (80%)
  local copies, waits for them, and re-layouts  6.91 us (19%)
    pallas_call x1, Pallas kernels, body(): pl.pallas_call(run, out_shape=jax.ShapeDtypeStruct((hard, share * rank_fu...  28.5 us
    unnamed x13, local copies, waits for them, and re-layouts  6.91 us

profile of v1, /device:TPU:0, one launch (start us, length us, event | category | flops | bytes accessed | tf_op | source)
XLA Modules:
  0.0 35.5 jit_solution(13994522525347951275)
XLA Ops:
  0.0 0.0 copy-start
  0.0 2.2 %copy-done = bf16[1024,2048]{1,0:T(8,128)(2,1)S(1)} copy-done((bf16[1024,2048]{1,0:T(8,128)(2,1)S(1)}, bf16[1024,2048]{1,0:T(8,128)(2,1)}, u32[]{:S(2)}) %copy-start) | copy-done | bytes 4194328
  2.2 0.0 copy-start.1
  2.2 1.2 %copy-done.1 = bf16[7168,64]{0,1:T(8,128)(2,1)S(1)} copy-done((bf16[7168,64]{0,1:T(8,128)(2,1)S(1)}, bf16[7168,64]{0,1:T(8,128)(2,1)}, u32[]{:S(2)}) %copy-start.1) | copy-done | bytes 917528
  3.4 0.0 copy-start.2
  3.4 0.9 %copy-done.2 = bf16[2048,64]{0,1:T(8,128)(2,1)S(1)} copy-done((bf16[2048,64]{0,1:T(8,128)(2,1)S(1)}, bf16[2048,64]{0,1:T(8,128)(2,1)}, u32[]{:S(2)}) %copy-start.2) | copy-done | bytes 262168
  4.3 0.0 copy-start.3
  4.3 0.7 %copy-done.3 = s32[1,16]{1,0:T(1,128)S(1)} copy-done((s32[1,16]{1,0:T(1,128)S(1)}, s32[1,16]{1,0:T(1,128)}, u32[]{:S(2)}) %copy-start.3) | copy-done | bytes 88
  5.0 0.0 copy-start.4
  5.0 0.7 %copy-done.4 = s32[1,8]{1,0:T(1,128)S(1)} copy-done((s32[1,8]{1,0:T(1,128)S(1)}, s32[1,8]{1,0:T(1,128)}, u32[]{:S(2)}) %copy-start.4) | copy-done | bytes 56
  5.6 0.0 copy-start.5
  5.6 0.7 %copy-done.5 = s32[8]{0:T(128)S(1)} copy-done((s32[8]{0:T(128)S(1)}, s32[8]{0:T(128)}, u32[]{:S(2)}) %copy-start.5) | copy-done | bytes 56
  6.3 28.5 %shard_map.73 = f32[8,2048]{1,0:T(8,128)S(1)} custom-call(bf16[1024,2048]{1,0:T(8,128)(2,1)S(1)} %copy-done, bf16[1024,7168]{1,0:T(8,128)(2,1)} %refs_1_.1, bf16[64,2048]{1,0:T(8,128)(2,1)S(1)} %bitcast.3, bf16[64,7168]{1,0:T(8,128)(2,1)S(1)} %bitcast.2, s32[1,16]{1,0:T(1,128)S(1)} %copy-done.3, s32[1,8]{1,0:T(1,128)S(1)} %copy-done.4, s32[8]{0:T(128)S(1)} %copy-done.5), custom_call_target="tpu_custom_call" | custom-call | flops 1207959552 | bytes 18874368 | tf_op jit(solution)/shard_map/pallas_call | solution.py:247
  34.8 0.6 %copy.9 = f32[8,2048]{1,0:T(8,128)} copy(f32[8,2048]{1,0:T(8,128)S(1)} %shard_map.73) | data formatting | bytes 131072
Async XLA Ops:
  0.0 2.2 %copy-start = (bf16[1024,2048]{1,0:T(8,128)(2,1)S(1)}, bf16[1024,2048]{1,0:T(8,128)(2,1)}, u32[]{:S(2)}) copy-start(bf16[1024,2048]{1,0:T(8,128)(2,1)} %refs_0_.1) | copy-start | bytes 12582916
  2.2 1.2 %copy-start.1 = (bf16[7168,64]{0,1:T(8,128)(2,1)S(1)}, bf16[7168,64]{0,1:T(8,128)(2,1)}, u32[]{:S(2)}) copy-start(bf16[7168,64]{0,1:T(8,128)(2,1)} %param.10) | copy-start | bytes 2752516
  3.4 0.9 %copy-start.2 = (bf16[2048,64]{0,1:T(8,128)(2,1)S(1)}, bf16[2048,64]{0,1:T(8,128)(2,1)}, u32[]{:S(2)}) copy-start(bf16[2048,64]{0,1:T(8,128)(2,1)} %param.9) | copy-start | bytes 786436
  4.3 0.7 %copy-start.3 = (s32[1,16]{1,0:T(1,128)S(1)}, s32[1,16]{1,0:T(1,128)}, u32[]{:S(2)}) copy-start(s32[1,16]{1,0:T(1,128)} %refs_4_.1) | copy-start | bytes 196
  5.0 0.7 %copy-start.4 = (s32[1,8]{1,0:T(1,128)S(1)}, s32[1,8]{1,0:T(1,128)}, u32[]{:S(2)}) copy-start(s32[1,8]{1,0:T(1,128)} %refs_5_.1) | copy-start | bytes 100
  5.6 0.7 %copy-start.5 = (s32[8]{0:T(128)S(1)}, s32[8]{0:T(128)}, u32[]{:S(2)}) copy-start(s32[8]{0:T(128)} %refs_6_.1) | copy-start | bytes 100

commit v2 on v1

--- a/solution.py
+++ b/solution.py
@@ -17,11 +17,11 @@
 
 def kernel(
     n_seq, n_sub, n_tp,
-    acts, grads, w_in, w_out, lengths, ids, slots,
+    acts, grads, w_in, w_out, lengths_in, ids_in, slots_in,
     out,
-    acts_v, grads_v, w_in_v, w_out_v,
+    acts_v, grads_v, w_in_v, w_out_v, lengths, ids, slots,
     a_own, a_got, g_own, g_got, acc, gath, slot_all,
-    load_sem, a_send, a_recv, g_send, g_recv, s_send, s_recv, f_send, f_recv, h_send,
+    load_sem, small_sem, a_send, a_recv, g_send, g_recv, s_send, s_recv, f_send, f_recv, h_send,
 ):
     seq, sub, tp = lax.axis_index("seq"), lax.axis_index("sub"), lax.axis_index("tp")
     ranks = n_seq * n_sub
@@ -42,6 +42,14 @@
         load_grads.append(
             pltpu.make_async_copy(grads.at[rows], grads_v.at[rows], load_sem.at[2 + chunks + c])
         )
+    small = [
+        pltpu.make_async_copy(source, target, small_sem.at[n])
+        for n, (source, target) in enumerate(
+            ((lengths_in, lengths), (ids_in, ids), (slots_in, slots))
+        )
+    ]
+    for copy in small:
+        copy.start()
     load_w_in.start()
     for copy in load_acts:
         copy.start()
@@ -62,6 +70,8 @@
             device_id={"seq": peer // n_sub, "sub": lax.rem(peer, n_sub)},
             device_id_type=MESH,
         )
+    for copy in small:
+        copy.wait()
     firsts = [jnp.int32(0)] * hard
     afters = [jnp.int32(0)] * hard
     chosen = [ids[0, k] for k in range(hard)]
@@ -238,8 +248,7 @@
     ranks = n_seq * n_sub
     f32 = jnp.float32
     dma = pltpu.SemaphoreType.DMA
-    hbm = pl.BlockSpec(memory_space=pl.ANY)
-    smem = pl.BlockSpec(memory_space=pltpu.SMEM)
+    hbm = pl.BlockSpec(memory_space=pltpu.HBM)
 
     def run(*refs):
         kernel(n_seq, n_sub, n_tp, *refs)
@@ -247,13 +256,16 @@
     return pl.pallas_call(
         run,
         out_shape=jax.ShapeDtypeStruct((hard, share * rank_full), f32),
-        in_specs=[hbm] * 4 + [smem] * 3,
+        in_specs=[hbm] * 7,
         out_specs=pl.BlockSpec(memory_space=pltpu.VMEM),
         scratch_shapes=[
             pltpu.VMEM((tokens, features), acts.dtype),
             pltpu.VMEM((tokens, hidden), grads.dtype),
             pltpu.VMEM(w_in.shape, w_in.dtype),
             pltpu.VMEM(w_out.shape, w_out.dtype),
+            pltpu.SMEM(lengths.shape, jnp.int32),
+            pltpu.SMEM(ids.shape, jnp.int32),
+            pltpu.SMEM(slots.shape, jnp.int32),
             pltpu.VMEM((chunks, n_tp, share, CHUNK), f32),
             pltpu.VMEM((n_tp - 1, chunks, share, CHUNK), f32),
             pltpu.VMEM((chunks, CHUNK // 2, 2 * rank_full), f32),
@@ -262,6 +274,7 @@
             pltpu.VMEM((ranks * hard, share * rank_full), f32),
             pltpu.VMEM((ranks, hard, -(-ranks * hard // 128) * 128), jnp.int32),
             dma((2 + 2 * chunks,)),
+            dma((3,)),
             dma((n_tp - 1, chunks)),
             dma((n_tp - 1, chunks)),
             dma((n_tp - 1, chunks)),
@@ -273,7 +286,7 @@
             dma((n_sub - 1, 2, n_seq)),
         ],
         compiler_params=pltpu.CompilerParams(
-            collective_id=0, has_side_effects=True, vmem_limit_bytes=48 * 2**20
+            collective_id=0, has_side_effects=True, vmem_limit_bytes=60 * 2**20
         ),
         cost_estimate=pl.CostEstimate(
             flops=2 * tokens * (features + hidden) * rank_full,

time: 35.7 us -> 29.8 us (0.83)
  local copies, waits for them, and re-layouts: 6.91 us -> 1.47 us
  Pallas kernels: 28.5 us -> 28.1 us
    unnamed x13 -> x1, local copies, waits for them, and re-layouts: 6.91 us -> 1.47 us
    pallas_call x1, Pallas kernels: 28.5 us -> 28.1 us  [body(): pl.pallas_call(run, out_shape=jax.ShapeDtypeStruct((hard, share * rank_fu...]
where the time goes in v2:
time: 29.8 us; the launch traced here: 29.6 us
  Pallas kernels  28.1 us (94%)
  local copies, waits for them, and re-layouts  1.47 us (5%)
    pallas_call x1, Pallas kernels, body(): pl.pallas_call(run, out_shape=jax.ShapeDtypeStruct((hard, share * rank_fu...  28.1 us
    unnamed x1, local copies, waits for them, and re-layouts  1.47 us

profile of v2, /device:TPU:0, one launch (start us, length us, event | category | flops | bytes accessed | tf_op | source)
XLA Modules:
  0.0 29.6 jit_solution(10967630371229225618)
XLA Ops:
  0.0 28.1 %shard_map.73 = f32[8,2048]{1,0:T(8,128)} custom-call(bf16[1024,2048]{1,0:T(8,128)(2,1)} %refs_0_.1, bf16[1024,7168]{1,0:T(8,128)(2,1)} %refs_1_.1, bf16[64,2048]{1,0:T(8,128)(2,1)} %bitcast.3, bf16[64,7168]{1,0:T(8,128)(2,1)} %bitcast.2, s32[1,16]{1,0:T(1,128)} %refs_4_.1, s32[1,8]{1,0:T(1,128)} %refs_5_.1, s32[8]{0:T(128)} %refs_6_.1), custom_call_target="tpu_custom_call" | custom-call | flops 1207959552 | bytes 18874368 | tf_op jit(solution)/shard_map/pallas_call | solution.py:256
  28.1 1.5 %copy.9 = f32[8,2048]{1,0:T(8,128)} copy(f32[8,2048]{1,0:T(8,128)} %shard_map.73) | data formatting | bytes 131072

commit v3 on v2

--- a/solution.py
+++ b/solution.py
@@ -7,6 +7,8 @@
 
 MESH = pl.DeviceIdType.MESH
 CHUNK = 256
+AHEAD = 9
+LOCAL = 0
 
 
 def project(rows, turned):
@@ -35,13 +37,22 @@
 
     load_w_in = pltpu.make_async_copy(w_in, w_in_v, load_sem.at[0])
     load_w_out = pltpu.make_async_copy(w_out, w_out_v, load_sem.at[1])
-    load_acts, load_grads = [], []
-    for c in range(chunks):
-        rows = pl.ds(c * CHUNK, CHUNK)
-        load_acts.append(pltpu.make_async_copy(acts.at[rows], acts_v.at[rows], load_sem.at[2 + c]))
-        load_grads.append(
-            pltpu.make_async_copy(grads.at[rows], grads_v.at[rows], load_sem.at[2 + chunks + c])
-        )
+    load_acts = [
+        pltpu.make_async_copy(
+            acts.at[pl.ds(c * CHUNK, CHUNK)],
+            acts_v.at[pl.ds(c * CHUNK, CHUNK)],
+            load_sem.at[2 + c],
+        )
+        for c in range(chunks)
+    ]
+    load_grads = [
+        pltpu.make_async_copy(
+            grads.at[pl.ds(c * half, half)],
+            grads_v.at[pl.ds(c * half, half)],
+            load_sem.at[2 + chunks + c],
+        )
+        for c in range(2 * chunks)
+    ]
     small = [
         pltpu.make_async_copy(source, target, small_sem.at[n])
         for n, (source, target) in enumerate(
@@ -50,12 +61,15 @@
     ]
     for copy in small:
         copy.start()
-    load_w_in.start()
-    for copy in load_acts:
+    order = [load_w_in, *load_acts, load_w_out, *load_grads]
+    for copy in order[:AHEAD]:
         copy.start()
-    load_w_out.start()
-    for copy in load_grads:
-        copy.start()
+
+    def take(n):
+        order[n].wait()
+        if n + AHEAD < len(order):
+            order[n + AHEAD].start()
+
 
     barrier = pltpu.get_barrier_semaphore()
     for d in range(1, n_tp):
@@ -87,30 +101,9 @@
     for k in range(hard):
         tile = jnp.where(tile_lane == rank * hard + k, slots[k], tile)
     slot_all[rank] = tile
-    pl.semaphore_wait(barrier, n_tp - 1 + ranks - 1)
-
-    slot_copies = []
-    for d in range(1, ranks):
-        peer = lax.rem(rank + d, ranks)
-        copy = pltpu.make_async_remote_copy(
-            src_ref=slot_all.at[rank],
-            dst_ref=slot_all.at[rank],
-            send_sem=s_send.at[d - 1],
-            recv_sem=s_recv.at[d - 1],
-            device_id={"seq": peer // n_sub, "sub": lax.rem(peer, n_sub)},
-            device_id_type=MESH,
-        )
-        copy.start()
-        slot_copies.append(copy)
-
-    a_copies, g_copies = [], []
-    load_w_in.wait()
-    for c in range(chunks):
-        load_acts[c].wait()
-        part = project(acts_v[c * CHUNK:(c + 1) * CHUNK, :], w_in_v[...])
-        turned = part.T
-        for q in range(n_tp):
-            a_own[c, q] = turned[q * share:(q + 1) * share, :]
+    a_copies, g_copies, slot_copies = [], [], []
+
+    def send_a(c):
         for d in range(1, n_tp):
             to = lax.rem(tp + d, n_tp)
             copy = pltpu.make_async_remote_copy(
@@ -123,11 +116,8 @@
             )
             copy.start()
             a_copies.append(copy)
-    load_w_out.wait()
-    for c in range(chunks):
-        load_grads[c].wait()
-        part = project(grads_v[c * CHUNK:(c + 1) * CHUNK, :], w_out_v[...])
-        g_own[c] = jnp.concatenate([part[:half], part[half:]], axis=1)
+
+    def send_g(c):
         for d in range(1, n_tp):
             copy = pltpu.make_async_remote_copy(
                 src_ref=g_own.at[c],
@@ -139,6 +129,42 @@
             )
             copy.start()
             g_copies.append(copy)
+
+    def enter():
+        pl.semaphore_wait(barrier, n_tp - 1 + ranks - 1)
+        for c in range(chunks):
+            send_a(c)
+        for c in range(LOCAL):
+            send_g(c)
+        for d in range(1, ranks):
+            peer = lax.rem(rank + d, ranks)
+            copy = pltpu.make_async_remote_copy(
+                src_ref=slot_all.at[rank],
+                dst_ref=slot_all.at[rank],
+                send_sem=s_send.at[d - 1],
+                recv_sem=s_recv.at[d - 1],
+                device_id={"seq": peer // n_sub, "sub": lax.rem(peer, n_sub)},
+                device_id_type=MESH,
+            )
+            copy.start()
+            slot_copies.append(copy)
+
+    take(0)
+    for c in range(chunks):
+        take(1 + c)
+        turned = project(acts_v[c * CHUNK:(c + 1) * CHUNK, :], w_in_v[...]).T
+        for q in range(n_tp):
+            a_own[c, q] = turned[q * share:(q + 1) * share, :]
+    take(1 + chunks)
+    for c in range(chunks):
+        if c == LOCAL:
+            enter()
+        for n in range(len(load_grads) // chunks):
+            take(2 + chunks + c * (len(load_grads) // chunks) + n)
+        part = project(grads_v[c * CHUNK:(c + 1) * CHUNK, :], w_out_v[...])
+        g_own[c] = jnp.concatenate([part[:half], part[half:]], axis=1)
+        if c >= LOCAL:
+            send_g(c)
 
     for copy in slot_copies:
         copy.wait()
@@ -273,7 +299,7 @@
             pltpu.VMEM((hard * share, 2 * rank_full), f32),
             pltpu.VMEM((ranks * hard, share * rank_full), f32),
             pltpu.VMEM((ranks, hard, -(-ranks * hard // 128) * 128), jnp.int32),
-            dma((2 + 2 * chunks,)),
+            dma((2 + 3 * chunks,)),
             dma((3,)),
             dma((n_tp - 1, chunks)),
             dma((n_tp - 1, chunks)),

time: 29.8 us -> 29.5 us (0.990)
  Pallas kernels: 28.1 us -> 27.8 us
where the time goes in v3:
time: 29.5 us; the launch traced here: 29.3 us
  Pallas kernels  27.8 us (94%)
  local copies, waits for them, and re-layouts  1.47 us (5%)
    pallas_call x1, Pallas kernels, body(): pl.pallas_call(run, out_shape=jax.ShapeDtypeStruct((hard, share * rank_fu...  27.8 us
    unnamed x1, local copies, waits for them, and re-layouts  1.47 us

profile of v3, /device:TPU:0, one launch (start us, length us, event | category | flops | bytes accessed | tf_op | source)
XLA Modules:
  0.0 29.3 jit_solution(11134211798061560441)
XLA Ops:
  0.0 27.8 %shard_map.73 = f32[8,2048]{1,0:T(8,128)} custom-call(bf16[1024,2048]{1,0:T(8,128)(2,1)} %refs_0_.1, bf16[1024,7168]{1,0:T(8,128)(2,1)} %refs_1_.1, bf16[64,2048]{1,0:T(8,128)(2,1)} %bitcast.3, bf16[64,7168]{1,0:T(8,128)(2,1)} %bitcast.2, s32[1,16]{1,0:T(1,128)} %refs_4_.1, s32[1,8]{1,0:T(1,128)} %refs_5_.1, s32[8]{0:T(128)} %refs_6_.1), custom_call_target="tpu_custom_call" | custom-call | flops 1207959552 | bytes 18874368 | tf_op jit(solution)/shard_map/pallas_call | solution.py:282
  27.8 1.5 %copy.9 = f32[8,2048]{1,0:T(8,128)} copy(f32[8,2048]{1,0:T(8,128)} %shard_map.73) | data formatting | bytes 131072
